TPU v7x, 256 devices: a whole 4x4x8 slice. The times are simulated.
256 devices in a mesh: facet: 64 (over z_lo, y, x, core), freq: 4 (over z_hi).
Axes of the slice: x: 4, y: 4, z: 8 (z_hi: 4, z_lo: 2; z = z_hi * 2 + z_lo), core: 2. Of those that a mesh axis runs over, the one named last changes fastest.
Arguments:
- visibility: bfloat16 [4, 2, 32768], P('freq', None, 'facet'), may hold values from -6 to 6
- row_target: int32 [4, 32768, 1], P('freq', 'facet'), may hold values from 0 to 63; in each aligned block of 512 rows (0 to 511, 512 to 1023, ..., all dimensions but the last counted through in order) at most 16 rows name the same one
- row_cell: int32 [4, 32768], P('freq', 'facet'), may hold values from 0 to 65535
- row_plane: int32 [4, 32768], P('freq', 'facet'), may hold values from 0 to 7
- kernel_table: bfloat16 [2, 2048, 256], replicated, may hold values from -3 to 3
- subgrid_anchor: int32 [64, 2], P('facet'), may hold values from 0 to 65535
Outputs:
- facet_image: float32 [65536, 128], P(('facet', 'freq'))
Inputs may be any that keep to these rules, and one draw needn't show every extreme that they name: `row_target`: among the rows of one device, at most 16 name any one subgrid.
All inputs are finite; a program needn't handle non-finite values.
Results may differ from a plain program's by a relative error of at most 0.006.
Values may be sent and summed in bfloat16 or wider, within the bound.
A program may use at most 128 MiB of HBM per device.

v0:
```python
import math

import jax
import jax.numpy as jnp
from jax import lax
from jax.sharding import PartitionSpec as P

NGRID = 65536
TROWS = 1024
TCOLS = 128


def phases(spatial, pixel):
    spatial_mod = spatial % NGRID
    pixel_mod = pixel % NGRID
    upper_part = pixel_mod // 256
    lower_part = pixel_mod % 256
    phase_index = (spatial_mod * upper_part % NGRID * 256 + spatial_mod * lower_part) % NGRID
    angles = phase_index.astype(jnp.float32) * (2.0 * math.pi / NGRID)
    return (jnp.cos(angles), jnp.sin(angles))


def grid_slots(values, packed, kernel_table):
    sub_size = kernel_table.shape[2]
    plane_cells = sub_size * sub_size
    w_plane = packed // plane_cells
    remainder = packed % plane_cells
    u_kernel = kernel_table[:, w_plane * sub_size + remainder // sub_size, :]
    v_kernel = kernel_table[:, w_plane * sub_size + remainder % sub_size, :].astype(jnp.float32)
    vis_real = values[0].astype(jnp.float32)[:, None]
    vis_imag = values[1].astype(jnp.float32)[:, None]
    term_real = (vis_real * v_kernel[0] - vis_imag * v_kernel[1]).astype(jnp.bfloat16)
    term_imag = (vis_real * v_kernel[1] + vis_imag * v_kernel[0]).astype(jnp.bfloat16)
    left_rows = jnp.concatenate([u_kernel[0], u_kernel[1]], axis=0)
    right_rows = jnp.concatenate(
        [
            jnp.concatenate([term_real, term_imag], axis=1),
            jnp.concatenate([-term_imag, term_real], axis=1),
        ],
        axis=0,
    )
    return lax.dot_general(
        left_rows, right_rows, (((0,), (0,)), ((), ())), preferred_element_type=jnp.float32
    )


def widened_block(block):
    half = block.shape[0]
    return jnp.concatenate(
        [block, jnp.concatenate([-block[:, half:], block[:, :half]], axis=1)], axis=0
    )


def tile_terms(widened, anchor_pair, facet_ids, tile_lines, scale):
    sub_size = widened.shape[0] // 2
    block_count = facet_ids.shape[0]
    spatial_u = anchor_pair[0] + jnp.arange(sub_size, dtype=jnp.int32)
    spatial_v = anchor_pair[1] + jnp.arange(sub_size, dtype=jnp.int32)
    pixels = (facet_ids // 8 * (NGRID // 8))[:, None] + tile_lines[None, :]
    cos_left, sin_left = phases(spatial_u[None, :], pixels.reshape(-1)[:, None])
    left_rows = jnp.concatenate([cos_left, sin_left], axis=1).astype(jnp.bfloat16)
    mixed = jnp.dot(left_rows, widened, preferred_element_type=jnp.float32).astype(jnp.bfloat16)
    columns = (facet_ids % 8 * (NGRID // 8))[:, None] + jnp.arange(TCOLS, dtype=jnp.int32)[None, :]
    cos_right, sin_right = phases(spatial_v[None, :, None], columns[:, None, :])
    right_rows = jnp.concatenate([cos_right, -sin_right], axis=1).astype(jnp.bfloat16)
    result = jnp.einsum(
        "bqc,bcn->bqn",
        mixed.reshape(block_count, -1, 2 * sub_size),
        right_rows,
        preferred_element_type=jnp.float32,
    )
    return result.reshape(-1, TCOLS) * scale


def shards(visibility, row_target, row_cell, row_plane, kernel_table, subgrid_anchor):
    facets = lax.axis_size("facet")
    bands = lax.axis_size("freq")
    rows_dev = visibility.shape[2]
    sub_size = kernel_table.shape[2]
    capacity = 2 * rows_dev // facets
    slot_count = facets * capacity
    scale = 1.0 / (sub_size * math.sqrt(facets * bands * rows_dev))
    destination = row_target[0, :, 0]
    onehot = (destination[:, None] == jnp.arange(facets, dtype=jnp.int32)[None, :]).astype(
        jnp.int32
    )
    position = jnp.sum(onehot * (jnp.cumsum(onehot, axis=0) - 1), axis=1)
    slot_index = destination * capacity + position
    sent_values = jnp.zeros((2, slot_count), jnp.bfloat16).at[:, slot_index].set(visibility[0])
    sent_cells = (
        jnp.zeros((1, slot_count), jnp.int32)
        .at[0, slot_index]
        .set(row_plane[0] * (sub_size * sub_size) + row_cell[0])
    )
    arrived = lax.all_to_all(sent_values, "facet", split_axis=1, concat_axis=1, tiled=True)
    arrived_cells = lax.all_to_all(sent_cells, "facet", split_axis=1, concat_axis=1, tiled=True)
    gridded = grid_slots(arrived, arrived_cells[0], kernel_table)
    subgrid = lax.psum(gridded, "freq").astype(jnp.bfloat16)
    band_index = lax.axis_index("freq")
    rows_band = TROWS // bands
    tile_lines = band_index * rows_band + jnp.arange(rows_band, dtype=jnp.int32)
    facet_index = lax.axis_index("facet")
    empty_tile = jnp.zeros((rows_band, TCOLS), jnp.float32)
    blocks = lax.all_gather(subgrid[None], "facet", axis=0, tiled=True)
    anchors = lax.all_gather(subgrid_anchor, "facet", axis=0, tiled=True)

    def add_member(member, carry):
        return carry + tile_terms(
            widened_block(blocks[member]), anchors[member], facet_index[None], tile_lines, scale
        )

    return lax.fori_loop(0, blocks.shape[0], add_member, empty_tile)


def solution(mesh):
    placed = (
        P("freq", None, "facet"),
        P("freq", "facet", None),
        P("freq", "facet"),
        P("freq", "facet"),
        P(),
        P("facet", None),
    )
    return jax.shard_map(
        shards, mesh=mesh, in_specs=placed, out_specs=P(("facet", "freq"), None), check_vma=False
    )
```

profile of v0, /device:TPU:8, one launch (start us, length us, event | category | flops | bytes accessed | tf_op | source)
XLA Modules:
  0.0 583.8 jit_solution(6002805119623340339)
XLA Ops:
  11.1 2.4 scatter_custom_fusion
  14.2 9.3 %all-to-all-start = ((s32[1,64,16]{2,0,1:T(1,128)}), s32[1,64,16]{2,0,1:T(1,128)S(1)}, u32[]{:S(2)}, u32[]{:S(2)}) async-start(s32[1,64,16]{2,0,1:T(1,128)} %bitcast.10), calls=%async_computation | async-start | bytes 65536 | tf_op jit(solution)/shard_map/all_to_all | solution.py:96
  24.4 1.8 scatter_custom_fusion.1
  27.3 3.2 all-to-all-done
  30.5 5.7 all-to-all-start.1
  37.7 5.6 all-to-all-done.1
  43.6 5.3 gather_fusion.1
  51.5 5.3 gather_fusion
  58.9 33.3 %all-reduce.2 = bf16[256,512]{1,0:T(8,128)(2,1)} all-reduce(f32[256,512]{1,0:T(8,128)S(1)} %fusion.42), channel_id=1, replica_groups=mesh['facet'=64,'freq'=4] {'freq'}, use_global_device_ids=true, to_apply=%region_5.6 | all-reduce | flops 131072 | bytes 786432 | tf_op jit(solution)/shard_map/psum | solution.py:98
  92.3 68.9 %all-gather.1 = s32[64,1,2]{2,1,0:T(1,128)S(1)} all-gather(s32[1,1,2]{2,1,0:T(1,128)S(1)} %bitcast.88), channel_id=1, replica_groups=mesh['facet'=64,'freq'=4] {'facet'}, dimensions={0}, use_global_device_ids=true | all-gather | bytes 520 | tf_op jit(solution)/shard_map/all_gather | solution.py:105
  161.3 52.4 %all-gather.4.cloned.1.call-done = bf16[16384,512]{1,0:T(8,128)(2,1)} async-done(((bf16[256,512]{1,0:T(8,128)(2,1)}), bf16[16384,512]{1,0:T(8,128)(2,1)}) %all-gather.4.cloned.1.call-update) | async-done | bytes 16777232 | tf_op jit(solution)/shard_map/all_gather | solution.py:104
  213.7 362.6 %while.17 = (s32[]{:T(128)}, f32[256,128]{1,0:T(8,128)S(1)}, s32[64,2]{0,1:T(2,128)S(1)}, s32[1]{0:T(128)}, bf16[64,256,512]{2,1,0:T(8,128)(2,1)}, /*index=5*/s32[1]{0:T(128)}, s32[]{:T(128)}, s32[]{:T(128)}, s32[]{:T(128)}) while((s32[]{:T(128)}, f32[256,128]{1,0:T(8,128)S(1)}, s32[64,2]{0,1:T(2,128)S(1)}, s32[1]{0:T(128)}, ...), condition=%wide.region_7.8_spmd.clone, body=%wide.region_6.7_spmd.clone.sunk | while | flops 173426560 | bytes 2631851 | solution.py:112
  216.3 1.5 cosine_convert_fusion.4
  222.0 1.5 cosine_convert_fusion.4
  233.3 1.5 cosine_convert_fusion.4
  244.7 1.5 cosine_convert_fusion.4
  250.3 1.5 cosine_convert_fusion.4
  261.7 1.5 cosine_convert_fusion.4
  267.3 1.5 cosine_convert_fusion.4
  273.0 1.5 cosine_convert_fusion.4
  278.7 1.5 cosine_convert_fusion.4
  290.0 1.5 cosine_convert_fusion.4
  295.7 1.5 cosine_convert_fusion.4
  312.7 1.5 cosine_convert_fusion.4
  (734 shorter events, 354.9 us)
Async XLA Ops:
  6.5 37.1 %copy-start = (bf16[2,2048,256]{2,1,0:T(8,128)(2,1)S(1)}, bf16[2,2048,256]{2,1,0:T(8,128)(2,1)}, u32[]{:S(2)}) copy-start(bf16[2,2048,256]{2,1,0:T(8,128)(2,1)} %param.12) | copy-start | bytes 6291460
  14.2 16.3 %all-to-all-start = ((s32[1,64,16]{2,0,1:T(1,128)}), s32[1,64,16]{2,0,1:T(1,128)S(1)}, u32[]{:S(2)}, u32[]{:S(2)}) async-start(s32[1,64,16]{2,0,1:T(1,128)} %bitcast.10), calls=%async_computation | async-start | bytes 65536 | tf_op jit(solution)/shard_map/all_to_all | solution.py:96
  30.5 12.8 %all-to-all-start.1 = ((bf16[2,64,16]{2,0,1:T(2,128)(2,1)}), bf16[2,64,16]{2,0,1:T(2,128)(2,1)S(1)}, u32[]{:S(2)}, u32[]{:S(2)}) async-start(bf16[2,64,16]{2,0,1:T(2,128)(2,1)} %copy.17), calls=%async_computation.1 | async-start | bytes 65536 | tf_op jit(solution)/shard_map/all_to_all | solution.py:95
  36.2 177.5 %all-gather.4.cloned.1.call-start = ((), (), s32[]{:S(2)}) async-start(), calls=%async_computation.2 | async-start | bytes 17039360 | tf_op jit(solution)/shard_map/all_gather | solution.py:104
  56.8 1.0 copy-start.1
  56.8 1.2 copy-start.2
  56.8 1.3 copy-start.3
  58.2 34.1 %copy-start.4 = (s32[1,2]{1,0:T(1,128)S(1)}, s32[1,2]{1,0:T(1,128)}, u32[]{:S(2)}) copy-start(s32[1,2]{1,0:T(1,128)} %param.13) | copy-start | bytes 28
  576.3 0.7 copy-start.5
Sparse Core Ops, SparseCore 0:
  92.4 121.2 all-gather.3
where the time goes:
time: 589 us; the launch traced here: 584 us
  other arithmetic  231 us (39%)
  local copies, waits for them, and re-layouts  126 us (21%)
  blocking collectives  102 us (17%)
  waiting for transfers between devices  61.3 us (10%)
  matrix products  31 us (5%)
  starting transfers between devices  15 us (3%)
  between operations  13.6 us (2%)
    another operation x130, other arithmetic  139 us
    select_n x128, other arithmetic, phases(): spatial_mod = spatial % NGRID  81 us
    all_gather x1, blocking collectives, shards(): anchors = lax.all_gather(subgrid_anchor, 'facet', axis=0, tiled=True)  68.9 us
    squeeze x64, local copies, waits for them, and re-layouts, add_member(): blocks[member]  62.3 us
    all_gather x1, waiting for transfers between devices, shards(): blocks = lax.all_gather(subgrid[None], 'facet', axis=0, tiled=True)  52.4 us
    slice x64, local copies, waits for them, and re-layouts, tile_terms(): spatial_v = anchor_pair[1] + jnp.arange(sub_size, dtype=jnp.int32)  38 us
    psum x1, blocking collectives, shards(): subgrid = lax.psum(gridded, 'freq').astype(jnp.bfloat16)  33.3 us
    dot_general x64, matrix products, tile_terms(): jnp.einsum('bqc,bcn->bqn', mixed.reshape(block_count, -1, 2 * sub_size),...  30.3 us
  transfers between devices with their start and end apart: 3, of which 3 were waited for; matrix products, arithmetic and copies ran while one was open for 1% of the time, Pallas kernels for 0%

commit v1 on v0

v1 whole, which is shorter than its diff:
```python
import functools
import math

import jax
import jax.numpy as jnp
from jax import lax
from jax.experimental import pallas as pl
from jax.experimental.pallas import tpu as pltpu
from jax.sharding import PartitionSpec as P

NGRID = 65536
TROWS = 1024
TCOLS = 128
SUB = 256
PLANES = 8
CAP = 16
RADIX = 8
LANES = 128
KS = SUB // RADIX
MESH = pl.DeviceIdType.MESH
F32, BF16, I32 = jnp.float32, jnp.bfloat16, jnp.int32


def turn(index):
    index = index & (NGRID - 1)
    quadrant = (index + NGRID // 8) >> 14
    rest = (index - (quadrant << 14)).astype(F32) * (2.0 * math.pi / NGRID)
    square = rest * rest
    sine = rest * (1.0 + square * (-1.0 / 6 + square * (1.0 / 120 + square * (-1.0 / 5040 + square * (1.0 / 362880)))))
    cosine = 1.0 + square * (-0.5 + square * (1.0 / 24 + square * (-1.0 / 720 + square * (1.0 / 40320))))
    odd = (quadrant & 1) == 1
    c = jnp.where(odd, sine, cosine)
    s = jnp.where(odd, cosine, sine)
    c = jnp.where(((quadrant + 1) & 2) == 2, -c, c)
    s = jnp.where((quadrant & 2) == 2, -s, s)
    return c, s


def iota(shape, dim):
    return lax.broadcasted_iota(I32, shape, dim)


def nt_dot(a, b):
    return lax.dot_general(a, b, (((1,), (1,)), ((), ())), preferred_element_type=F32)


def tn_dot(a, b):
    return lax.dot_general(a, b, (((0,), (0,)), ((), ())), preferred_element_type=F32)


def dot(a, b):
    return jnp.dot(a, b, preferred_element_type=F32)


def kernel(
    facets, bands, scale,
    vis_ref, target_ref, cell_ref, plane_ref, anchor_ref, table_hbm, out_ref,
    table, send1, recv1, right, send2, recv2, left, send3, recv3, send4, recv4,
    table_sem, send_sems, recv_sems,
):
    me = lax.axis_index("facet")
    band = lax.axis_index("freq")
    my_class, my_column = me // RADIX, me % RADIX
    rows = vis_ref.shape[1]
    cells = PLANES * SUB
    band_rows = TROWS // bands

    load_table = pltpu.make_async_copy(table_hbm, table, table_sem)
    load_table.start()

    barrier = pltpu.get_barrier_semaphore()

    @pl.loop(1, facets)
    def _(offset):
        pl.semaphore_signal(
            barrier, inc=1, device_id={"facet": lax.rem(me + offset, facets)}, device_id_type=MESH
        )

    for offset in range(1, bands):
        pl.semaphore_signal(
            barrier, inc=1, device_id={"freq": lax.rem(band + offset, bands)}, device_id_type=MESH
        )

    named = iota((facets, rows), 0) == target_ref[...]
    named_f = jnp.where(named, 1.0, 0.0)
    named_b = named_f.astype(BF16)
    earlier = jnp.where(iota((rows, rows), 0) < iota((rows, rows), 1), 1.0, 0.0).astype(BF16)
    position = jnp.sum(named_f * dot(named_b, earlier), axis=0, keepdims=True)
    here = iota((CAP, rows), 0).astype(F32) == position
    vis = vis_ref[...].astype(F32)
    cell = cell_ref[...]
    payloads = (
        vis[0:1], vis[1:2], (cell >> 8).astype(F32), (cell & 255).astype(F32), plane_ref[...].astype(F32),
    )
    spread = [jnp.where(here, payload, 0.0) for payload in payloads]
    spread.append(jnp.zeros((LANES - CAP * len(payloads), rows), F32))
    slots = nt_dot(named_b, jnp.concatenate(spread, axis=0).astype(BF16))
    lane = iota((facets, LANES), 1)
    us, vs = anchor_ref[0, 0], anchor_ref[0, 1]
    slots = jnp.where(lane == CAP * 5, us.astype(F32), slots)
    send1[...] = slots.reshape(facets, 1, LANES)
    recv1[pl.ds(me, 1)] = send1[pl.ds(me, 1)]

    pl.semaphore_wait(barrier, facets - 1 + bands - 1)

    @pl.loop(1, facets)
    def _(offset):
        peer = lax.rem(me + offset, facets)
        pltpu.make_async_remote_copy(
            src_ref=send1.at[peer], dst_ref=recv1.at[me], send_sem=send_sems.at[0], recv_sem=recv_sems.at[0],
            device_id={"facet": peer}, device_id_type=MESH,
        ).start()

    def settle(source, target, phase, axis, count, amount):
        return pltpu.make_async_remote_copy(
            src_ref=source.at[pl.ds(0, amount)], dst_ref=target.at[pl.ds(0, amount)],
            send_sem=send_sems.at[phase], recv_sem=recv_sems.at[phase],
            device_id={axis: lax.rem(lax.axis_index(axis) + 1, count)}, device_id_type=MESH,
        )

    for group in range(RADIX):
        spatial = vs + iota((SUB, TCOLS), 0)
        pixel = iota((SUB, TCOLS), 1)
        index = (((spatial & (RADIX - 1)) * group & (RADIX - 1)) << 13) + spatial * pixel
        cos_r, sin_r = turn(index)
        cos_r, sin_r = cos_r.astype(BF16), sin_r.astype(BF16)
        right[group, :SUB, :TCOLS] = cos_r
        right[group, :SUB, TCOLS:] = sin_r
        right[group, SUB:, :TCOLS] = -sin_r
        right[group, SUB:, TCOLS:] = cos_r

    load_table.wait()
    wait1 = settle(send1, recv1, 0, "facet", facets, facets - 1)
    wait1.wait_recv()

    got = recv1[...].reshape(facets, LANES)
    u_cell = got[:, 2 * CAP:3 * CAP] + got[:, 4 * CAP:5 * CAP] * SUB
    v_cell = got[:, 3 * CAP:4 * CAP] + got[:, 4 * CAP:5 * CAP] * SUB
    every = iota((facets, cells), 1).astype(F32)

    def picker(values):
        return jnp.concatenate(
            [jnp.where(every == values[:, q:q + 1], 1.0, 0.0).astype(BF16) for q in range(CAP)], axis=0
        )

    pick_u, pick_v = picker(u_cell), picker(v_cell)
    a_real = dot(pick_u, table[0]).astype(BF16)
    a_imag = dot(pick_u, table[1]).astype(BF16)
    k_real = dot(pick_v, table[0])
    k_imag = dot(pick_v, table[1])
    v_real = jnp.concatenate([got[:, q:q + 1] for q in range(CAP)], axis=0)
    v_imag = jnp.concatenate([got[:, CAP + q:CAP + q + 1] for q in range(CAP)], axis=0)
    b_real = (v_real * k_real - v_imag * k_imag).astype(BF16)
    b_imag = (v_real * k_imag + v_imag * k_real).astype(BF16)
    b_wide = jnp.concatenate([b_real, b_imag], axis=1)
    b_turned = jnp.concatenate([-b_imag, b_real], axis=1)
    grid = (tn_dot(a_real, b_wide) + tn_dot(a_imag, b_turned)).astype(BF16)
    place = iota((SUB, SUB), 0)
    wanted = ((place & (KS - 1)) << 3) + (((place >> 5) - us) & (RADIX - 1))
    order = jnp.where(iota((SUB, SUB), 1) == wanted, 1.0, 0.0).astype(BF16)
    grid = dot(order, grid).astype(BF16)

    @pl.loop(0, RADIX)
    def _(step):
        column = lax.rem(my_column + step, RADIX)
        half = dot(grid, right[column]).astype(BF16)
        for c in range(RADIX):
            send2[c * RADIX + column] = half[c * KS:(c + 1) * KS]

        @pl.loop(0, RADIX)
        def _(turn_by):
            peer = lax.rem(my_class + turn_by, RADIX) * RADIX + column

            @pl.when(peer != me)
            def _():
                pltpu.make_async_remote_copy(
                    src_ref=send2.at[peer], dst_ref=recv2.at[me],
                    send_sem=send_sems.at[1], recv_sem=recv_sems.at[1],
                    device_id={"facet": peer}, device_id_type=MESH,
                ).start()

    recv2[pl.ds(me, 1)] = send2[pl.ds(me, 1)]

    width = facets * KS
    own_s = iota((facets, width), 0) == (iota((facets, width), 1) >> 5)
    first = jnp.sum(jnp.where(own_s, got[:, 5 * CAP:5 * CAP + 1], 0.0), axis=0, keepdims=True).astype(I32)
    first = first + ((my_class - first) & (RADIX - 1))
    spatial = first + ((iota((1, width), 1) & (KS - 1)) << 3)
    fine = 32
    coarse_r, coarse_i = turn(iota((TROWS // fine, width), 0) * fine * spatial)
    fine_r, fine_i = turn(iota((fine, width), 0) * spatial)
    for piece in range(TROWS // fine):
        p_r, p_i = coarse_r[piece:piece + 1], coarse_i[piece:piece + 1]
        base = piece * fine
        block = base // band_rows
        at = base % band_rows
        left[block, at:at + fine] = (p_r * fine_r - p_i * fine_i).astype(BF16)
        left[block, band_rows + at:band_rows + at + fine] = (p_r * fine_i + p_i * fine_r).astype(BF16)

    wait2 = settle(send2, recv2, 1, "facet", facets, facets - 1)
    wait2.wait_recv()

    mixed = recv2[...].reshape(width, 2 * TCOLS)

    def tile_part(block):
        both = dot(left[block], mixed)
        upper, lower = both[:band_rows], both[band_rows:]
        return jnp.concatenate(
            [upper[:, :TCOLS] - lower[:, TCOLS:], upper[:, TCOLS:] + lower[:, :TCOLS]], axis=1
        )

    offsets = [2, 1, 3][:bands - 1]
    for offset in offsets:
        other = lax.rem(band + offset, bands)
        send3[offset - 1] = tile_part(other).astype(BF16)
        pltpu.make_async_remote_copy(
            src_ref=send3.at[offset - 1], dst_ref=recv3.at[offset - 1],
            send_sem=send_sems.at[2], recv_sem=recv_sems.at[2],
            device_id={"freq": other}, device_id_type=MESH,
        ).start()
    total = tile_part(band)
    wait3 = settle(send3, recv3, 2, "freq", bands, bands - 1)
    wait3.wait_recv()
    for offset in offsets:
        total = total + recv3[offset - 1].astype(F32)
    t_real, t_imag = total[:, :TCOLS], total[:, TCOLS:]

    def turned(other):
        angle = jnp.zeros((1, TCOLS), I32) + ((my_class * other & (RADIX - 1)) << 13)
        cos_c, sin_c = turn(angle)
        return t_real * cos_c - t_imag * sin_c

    for offset in range(1, RADIX):
        other = lax.rem(my_class + offset, RADIX)
        send4[offset - 1] = turned(other).astype(BF16)
        pltpu.make_async_remote_copy(
            src_ref=send4.at[offset - 1], dst_ref=recv4.at[offset - 1],
            send_sem=send_sems.at[3], recv_sem=recv_sems.at[3],
            device_id={"facet": other * RADIX + my_column}, device_id_type=MESH,
        ).start()
    image = turned(my_class)
    wait4 = settle(send4, recv4, 3, "facet", facets, RADIX - 1)
    wait4.wait_recv()
    for offset in range(1, RADIX):
        image = image + recv4[offset - 1].astype(F32)
    out_ref[...] = image * scale

    for finished in (wait1, wait2, wait3, wait4):
        finished.wait_send()


def shards(visibility, row_target, row_cell, row_plane, kernel_table, subgrid_anchor):
    facets = lax.axis_size("facet")
    bands = lax.axis_size("freq")
    rows = visibility.shape[2]
    scale = 1.0 / (SUB * math.sqrt(facets * bands * rows))
    width = facets * KS
    band_rows = TROWS // bands
    vmem = pl.BlockSpec(memory_space=pltpu.VMEM)
    return pl.pallas_call(
        functools.partial(kernel, facets, bands, scale),
        out_shape=jax.ShapeDtypeStruct((band_rows, TCOLS), F32),
        in_specs=[vmem, vmem, vmem, vmem, pl.BlockSpec(memory_space=pltpu.SMEM), pl.BlockSpec(memory_space=pl.ANY)],
        out_specs=vmem,
        scratch_shapes=[
            pltpu.VMEM((2, PLANES * SUB, SUB), BF16),
            pltpu.VMEM((facets, 1, LANES), F32),
            pltpu.VMEM((facets, 1, LANES), F32),
            pltpu.VMEM((RADIX, 2 * SUB, 2 * TCOLS), BF16),
            pltpu.VMEM((facets, KS, 2 * TCOLS), BF16),
            pltpu.VMEM((facets, KS, 2 * TCOLS), BF16),
            pltpu.VMEM((bands, 2 * band_rows, width), BF16),
            pltpu.VMEM((bands - 1, band_rows, 2 * TCOLS), BF16),
            pltpu.VMEM((bands - 1, band_rows, 2 * TCOLS), BF16),
            pltpu.VMEM((RADIX - 1, band_rows, TCOLS), BF16),
            pltpu.VMEM((RADIX - 1, band_rows, TCOLS), BF16),
            pltpu.SemaphoreType.DMA,
            pltpu.SemaphoreType.DMA((4,)),
            pltpu.SemaphoreType.DMA((4,)),
        ],
        compiler_params=pltpu.CompilerParams(
            collective_id=0, has_side_effects=True, vmem_limit_bytes=60 * 1024 * 1024
        ),
        cost_estimate=pl.CostEstimate(flops=8 * 10**9, bytes_accessed=4 * 10**6, transcendentals=0),
    )(
        visibility[0], row_target.reshape(1, rows), row_cell, row_plane, subgrid_anchor, kernel_table
    )


def solution(mesh):
    placed = (
        P("freq", None, "facet"),
        P("freq", "facet", None),
        P("freq", "facet"),
        P("freq", "facet"),
        P(),
        P("facet", None),
    )
    return jax.shard_map(
        shards, mesh=mesh, in_specs=placed, out_specs=P(("facet", "freq"), None), check_vma=False
    )
```

time: 589 us -> 65.6 us (0.11)
  the two profiles are of different devices: /device:TPU:8 before, /device:TPU:1 now
where the time goes in v1:
time: 65.6 us; the launch traced here: 65.5 us
  Pallas kernels  63.9 us (97%)
  local copies, waits for them, and re-layouts  1.57 us (2%)
    pallas_call x1, Pallas kernels, shards(): pl.pallas_call(functools.partial(kernel, facets, bands, scale), out_shape...  63.9 us
    unnamed x1, local copies, waits for them, and re-layouts  1.57 us

profile of v1, /device:TPU:1, one launch (start us, length us, event | category | flops | bytes accessed | tf_op | source)
XLA Modules:
  0.0 65.5 jit_solution(8495630078582088001)
XLA Ops:
  0.0 63.9 %shard_map.64 = f32[256,128]{1,0:T(8,128)} custom-call(bf16[2,512]{1,0:T(2,128)(2,1)} %bitcast.2, s32[1,512]{1,0:T(1,128)} %bitcast.3, s32[1,512]{1,0:T(1,128)} %cell_ref.1, s32[1,512]{1,0:T(1,128)} %plane_ref.1, s32[1,2]{1,0:T(1,128)} %anchor_ref.1, bf16[2,2048,256]{2,1,0:T(8,128)(2,1)} %table_hbm.1), custom_call_target="tpu_custom_call" | custom-call | flops 8000000000 | bytes 4000000 | tf_op jit(solution)/shard_map/pallas_call | solution.py:260
  63.9 1.6 %copy.8 = f32[256,128]{1,0:T(8,128)} copy(f32[256,128]{1,0:T(8,128)} %shard_map.64) | data formatting | bytes 262144

commit v2 on v1

v2 whole, which is shorter than its diff:
```python
import functools
import math

import jax
import jax.numpy as jnp
from jax import lax
from jax.experimental import pallas as pl
from jax.experimental.pallas import tpu as pltpu
from jax.sharding import PartitionSpec as P

NGRID = 65536
TROWS = 1024
TCOLS = 128
SUB = 256
PLANES = 8
CAP = 16
RADIX = 8
LANES = 128
KS = SUB // RADIX
SECTIONS = 2
MESH = pl.DeviceIdType.MESH
F32, BF16, I32 = jnp.float32, jnp.bfloat16, jnp.int32


def turn(index):
    index = index & (NGRID - 1)
    quadrant = (index + NGRID // 8) >> 14
    rest = (index - (quadrant << 14)).astype(F32) * (2.0 * math.pi / NGRID)
    square = rest * rest
    sine = rest * (1.0 + square * (-1.0 / 6 + square * (1.0 / 120 + square * (-1.0 / 5040 + square * (1.0 / 362880)))))
    cosine = 1.0 + square * (-0.5 + square * (1.0 / 24 + square * (-1.0 / 720 + square * (1.0 / 40320))))
    odd = (quadrant & 1) == 1
    c = jnp.where(odd, sine, cosine)
    s = jnp.where(odd, cosine, sine)
    c = jnp.where(((quadrant + 1) & 2) == 2, -c, c)
    s = jnp.where((quadrant & 2) == 2, -s, s)
    return c, s


def iota(shape, dim):
    return lax.broadcasted_iota(I32, shape, dim)


def nt_dot(a, b):
    return lax.dot_general(a, b, (((1,), (1,)), ((), ())), preferred_element_type=F32)


def tn_dot(a, b):
    return lax.dot_general(a, b, (((0,), (0,)), ((), ())), preferred_element_type=F32)


def dot(a, b):
    return jnp.dot(a, b, preferred_element_type=F32)


def send(source, target, send_sem, recv_sem, device):
    copy = pltpu.make_async_remote_copy(
        src_ref=source, dst_ref=target, send_sem=send_sem, recv_sem=recv_sem,
        device_id=device, device_id_type=MESH,
    )
    copy.start()
    return copy


class RingSum:
    def __init__(self, chunk, up, down, out_ref, in_ref, send_sem, recv_sem):
        self.chunk, self.up, self.down = chunk, up, down
        self.out, self.came, self.send_sem, self.recv_sem = out_ref, in_ref, send_sem, recv_sem
        self.copies = []

    def go(self, slot, value, device):
        self.out[slot] = value.astype(BF16)
        copy = send(self.out.at[slot], self.came.at[slot], self.send_sem.at[slot], self.recv_sem.at[slot], device)
        self.copies.append(copy)

    def arrived(self, slot):
        self.copies[slot].wait_recv()
        return self.came[slot].astype(F32)

    def start(self):
        self.go(0, self.chunk(2, 0), self.up)
        self.go(1, self.chunk(2, 1), self.down)

    def plain(self):
        self.go(2, self.chunk(1, 1), self.up)
        self.go(3, self.chunk(3, 0), self.down)

    def middle(self):
        term_up, term_down = self.chunk(1, 0), self.chunk(3, 1)
        self.go(4, term_up + self.arrived(0), self.up)
        self.go(5, term_down + self.arrived(1), self.down)

    def finish(self):
        halves = [self.chunk(0, 0), self.chunk(0, 1)]
        halves = [halves[0] + self.arrived(3), halves[1] + self.arrived(2)]
        halves = [halves[0] + self.arrived(4), halves[1] + self.arrived(5)]
        return jnp.concatenate(halves, axis=0)


def kernel(
    facets, bands, scale,
    vis_ref, target_ref, cell_ref, plane_ref, anchor_ref, table_hbm, out_ref,
    table, ordered, send1, recv1, right, grid_out, grid_in, send2, recv2, left, part_out, part_in, last_out, last_in,
    table_sem, send_sems, recv_sems, grid_sems, part_sems, last_sems,
):
    me = lax.axis_index("facet")
    band = lax.axis_index("freq")
    my_class, my_column = me // RADIX, me % RADIX
    my_z, my_y = my_class // 4, my_class % 4
    rows = vis_ref.shape[1]
    cells = PLANES * SUB
    band_rows = TROWS // bands
    kept = KS // bands
    band_up = {"freq": lax.rem(band + 1, bands)}
    band_down = {"freq": lax.rem(band + bands - 1, bands)}

    load_table = pltpu.make_async_copy(table_hbm, table, table_sem)
    load_table.start()

    barrier = pltpu.get_barrier_semaphore()

    @pl.loop(1, facets)
    def _(offset):
        pl.semaphore_signal(
            barrier, inc=1, device_id={"facet": lax.rem(me + offset, facets)}, device_id_type=MESH
        )

    pl.semaphore_signal(barrier, inc=1, device_id=band_up, device_id_type=MESH)
    pl.semaphore_signal(barrier, inc=1, device_id=band_down, device_id_type=MESH)

    named = iota((facets, rows), 0) == target_ref[...]
    named_f = jnp.where(named, 1.0, 0.0)
    named_b = named_f.astype(BF16)
    earlier = jnp.where(iota((rows, rows), 0) < iota((rows, rows), 1), 1.0, 0.0).astype(BF16)
    position = jnp.sum(named_f * dot(named_b, earlier), axis=0, keepdims=True)
    here = iota((CAP, rows), 0).astype(F32) == position
    vis = vis_ref[...].astype(F32)
    cell = cell_ref[...]
    payloads = (
        vis[0:1], vis[1:2], (cell >> 8).astype(F32), (cell & 255).astype(F32), plane_ref[...].astype(F32),
    )
    spread = [jnp.where(here, payload, 0.0) for payload in payloads]
    spread.append(jnp.zeros((LANES - CAP * len(payloads), rows), F32))
    slots = nt_dot(named_b, jnp.concatenate(spread, axis=0).astype(BF16))
    lane = iota((facets, LANES), 1)
    us, vs = anchor_ref[0, 0], anchor_ref[0, 1]
    slots = jnp.where(lane == CAP * 5, us.astype(F32), slots)
    send1[...] = slots.reshape(facets, 1, LANES)
    recv1[pl.ds(me, 1)] = send1[pl.ds(me, 1)]

    pl.semaphore_wait(barrier, facets - 1 + 2)

    @pl.loop(1, facets)
    def _(offset):
        peer = lax.rem(me + offset, facets)
        send(send1.at[peer], recv1.at[me], send_sems.at[0], recv_sems.at[0], {"facet": peer})

    def settle(target, phase):
        return pltpu.make_async_remote_copy(
            src_ref=target.at[pl.ds(0, facets - 1)], dst_ref=target.at[pl.ds(0, facets - 1)],
            send_sem=send_sems.at[phase], recv_sem=recv_sems.at[phase],
            device_id={"facet": lax.rem(me + 1, facets)}, device_id_type=MESH,
        )

    for step in range(RADIX):
        group = lax.rem(my_column + step, RADIX)
        spatial = vs + iota((SUB, TCOLS), 0)
        pixel = iota((SUB, TCOLS), 1)
        index = (((spatial & (RADIX - 1)) * group & (RADIX - 1)) << 13) + spatial * pixel
        cos_r, sin_r = turn(index)
        cos_r, sin_r = cos_r.astype(BF16), sin_r.astype(BF16)
        at = step * 2 * TCOLS
        right[:SUB, at:at + TCOLS] = cos_r
        right[:SUB, at + TCOLS:at + 2 * TCOLS] = sin_r
        right[SUB:, at:at + TCOLS] = -sin_r
        right[SUB:, at + TCOLS:at + 2 * TCOLS] = cos_r

    load_table.wait()
    place = iota((SUB, SUB), 0)
    row_k = (((place >> 6) + band) & (bands - 1)) * kept + (place & (kept - 1))
    wanted = (row_k << 3) + ((((place >> 3) & (RADIX - 1)) - us) & (RADIX - 1))
    order = jnp.where(iota((SUB, SUB), 1) == wanted, 1.0, 0.0).astype(BF16)
    for part in range(2):
        ordered[part * SUB:(part + 1) * SUB] = nt_dot(order, table[part]).astype(BF16)

    wait1 = settle(recv1, 0)
    wait1.wait_recv()

    got = recv1[...].reshape(facets, LANES)
    v_cell = got[:, 3 * CAP:4 * CAP] + got[:, 4 * CAP:5 * CAP] * SUB
    every = iota((facets, cells), 1).astype(F32)
    pick_v = jnp.concatenate(
        [jnp.where(every == v_cell[:, q:q + 1], 1.0, 0.0).astype(BF16) for q in range(CAP)], axis=0
    )
    k_real = dot(pick_v, table[0])
    k_imag = dot(pick_v, table[1])
    v_real = jnp.concatenate([got[:, q:q + 1] for q in range(CAP)], axis=0)
    v_imag = jnp.concatenate([got[:, CAP + q:CAP + q + 1] for q in range(CAP)], axis=0)
    b_real = (v_real * k_real - v_imag * k_imag).astype(BF16)
    b_imag = (v_real * k_imag + v_imag * k_real).astype(BF16)
    flat = got.T
    u_row = jnp.concatenate([flat[2 * CAP + q:2 * CAP + q + 1] for q in range(CAP)], axis=1)
    plane_row = jnp.concatenate([flat[4 * CAP + q:4 * CAP + q + 1] for q in range(CAP)], axis=1)
    pick_u = jnp.where(iota((SUB, facets * CAP), 0).astype(F32) == u_row, 1.0, 0.0).astype(BF16)
    pick_u = jnp.concatenate(
        [pick_u * jnp.where(plane_row == p, 1.0, 0.0).astype(BF16) for p in range(PLANES)], axis=0
    )
    a_both = dot(ordered[...], pick_u).astype(BF16)
    b_wide = jnp.concatenate([b_real, b_imag], axis=1)
    b_turned = jnp.concatenate([-b_imag, b_real], axis=1)
    quarter = SUB // bands
    gridded = dot(a_both[:SUB], b_wide) + dot(a_both[SUB:], b_turned)

    def grid_chunk(r, h):
        start = r * quarter + h * (quarter // 2)
        return gridded[start:start + quarter // 2]

    width = facets * 2 * kept
    own_s = iota((facets, width), 0) == (iota((facets, width), 1) >> 4)
    first = jnp.sum(jnp.where(own_s, got[:, 5 * CAP:5 * CAP + 1], 0.0), axis=0, keepdims=True).astype(I32)
    first = first + ((my_class - first) & (RADIX - 1))
    column = iota((1, width), 1)
    spatial = first + (((column & (kept - 1)) + band * kept) << 3)
    ahead = ((column >> 3) & 1) << 14
    fine = 32
    pieces = band_rows // fine
    coarse = iota((bands * pieces, width), 0)
    coarse = ((((coarse >> 3) + band) & (bands - 1)) << 3) + (coarse & (pieces - 1))

    def make_left(blocks):
        for piece in range(blocks[0] * pieces, (blocks[-1] + 1) * pieces):
            p_r, p_i = coarse_r[piece:piece + 1], coarse_i[piece:piece + 1]
            block, at = piece // pieces, piece % pieces * fine
            left[block, 0, at:at + fine] = (p_r * fine_r - p_i * fine_i).astype(BF16)
            left[block, 1, at:at + fine] = (p_r * fine_i + p_i * fine_r).astype(BF16)

    ring = RingSum(grid_chunk, band_up, band_down, grid_out, grid_in, grid_sems.at[0], grid_sems.at[1])
    ring.start()
    ring.plain()
    coarse_r, coarse_i = turn(coarse * fine * spatial)
    fine_r, fine_i = turn(iota((fine, width), 0) * spatial + ahead)
    ring.middle()
    make_left(range(bands))
    grid = ring.finish().astype(BF16)

    share = RADIX // 2
    for part in range(2):
        span = share * 2 * TCOLS
        half = dot(grid, right[:, part * span:(part + 1) * span])
        for step in range(share):
            at = step * 2 * TCOLS
            pieces = [half[:, at + p * TCOLS:at + (p + 1) * TCOLS].reshape(RADIX, kept, TCOLS) for p in range(2)]
            send2[part * share + step] = jnp.concatenate(pieces, axis=1).astype(BF16)

        @pl.loop(0, share * RADIX)
        def _(number):
            step, turn_by = part * share + number // RADIX, number % RADIX
            peer_class = lax.rem(my_class + turn_by, RADIX)
            peer = peer_class * RADIX + lax.rem(my_column + step, RADIX)

            @pl.when(peer != me)
            def _():
                send(send2.at[step, peer_class], recv2.at[me], send_sems.at[1], recv_sems.at[1], {"facet": peer})

    recv2[pl.ds(me, 1)] = send2[0, pl.ds(my_class, 1)]

    wait2 = settle(recv2, 1)
    wait2.wait_recv()

    mixed = recv2[...].reshape(width, TCOLS)
    sections = part_out.shape[0]
    section_rows = band_rows // sections
    half_rows = section_rows // 2
    y_up, y_down = lax.rem(my_y + 1, 4), lax.rem(my_y + 3, 4)
    across = lax.rem(my_y + 2, 4)

    def tile_part(section, r, h):
        at = section * section_rows + h * half_rows
        return jnp.concatenate([dot(left[r, p, at:at + half_rows], mixed) for p in range(2)], axis=1)

    def phase(z, y):
        return turn(jnp.zeros((1, TCOLS), I32) + ((my_class * (4 * z + y) & (RADIX - 1)) << 13))

    phases = {(z, n): phase(z, y) for z in range(2) for n, y in enumerate((my_y, y_up, across, y_down))}
    phases["pair"], phases["own"] = phase(1 - my_z, my_y), phase(my_z, my_y)

    class Last:
        def __init__(self, section, total):
            self.real, self.imag = total[:, :TCOLS], total[:, TCOLS:]
            self.out, self.came = last_out.at[section], last_in.at[section]
            self.send_sem, self.recv_sem = last_sems.at[0, section], last_sems.at[1, section]
            self.copies = []

        def turned(self, key):
            return self.real * phases[key][0] - self.imag * phases[key][1]

        def go(self, out_slot, in_slot, value, z, y):
            self.out[out_slot] = value.astype(BF16)
            copy = send(
                self.out.at[out_slot], self.came.at[in_slot], self.send_sem.at[out_slot], self.recv_sem.at[in_slot],
                {"facet": (z * 4 + y) * RADIX + my_column},
            )
            self.copies.append(copy)

        def arrived(self, slot):
            pltpu.make_async_remote_copy(
                src_ref=self.out.at[slot], dst_ref=self.came.at[slot], send_sem=self.send_sem.at[slot],
                recv_sem=self.recv_sem.at[slot], device_id={"facet": lax.rem(me + 1, facets)}, device_id_type=MESH,
            ).wait_recv()
            return self.came[slot].astype(F32)

        def start(self):
            self.go(0, 0, self.turned((0, 2)), my_z, y_up)
            self.go(1, 1, self.turned((1, 2)), my_z, y_down)
            self.go(2, 2 + my_z, self.turned((1, 1)), 1, y_up)
            self.go(3, 4 + my_z, self.turned((0, 3)), 0, y_down)
            self.go(6, 6, self.turned("pair"), 1 - my_z, my_y)

        def middle(self):
            term_up, term_down = self.turned((0, 1)), self.turned((1, 3))
            self.go(4, 2 + my_z, term_up + self.arrived(0), 0, y_up)
            self.go(5, 4 + my_z, term_down + self.arrived(1), 1, y_down)

        def finish(self):
            image = self.turned("own")
            for slot in range(2, 7):
                image = image + self.arrived(slot)
            return image

    rings = [
        RingSum(
            functools.partial(tile_part, section), band_up, band_down,
            part_out.at[section], part_in.at[section], part_sems.at[0, section], part_sems.at[1, section],
        )
        for section in range(sections)
    ]
    for each in rings:
        each.start()
    for each in rings:
        each.plain()
    for each in rings:
        each.middle()
    lasts = []
    for section, each in enumerate(rings):
        lasts.append(Last(section, each.finish()))
        lasts[-1].start()
        if section:
            lasts[section - 1].middle()
    lasts[-1].middle()
    for section, each in enumerate(lasts):
        out_ref[section * section_rows:(section + 1) * section_rows] = each.finish() * scale

    for finished in [wait1, wait2]:
        finished.wait_send()
    for each in [ring, *rings, *lasts]:
        for copy in each.copies:
            copy.wait_send()


def shards(visibility, row_target, row_cell, row_plane, kernel_table, subgrid_anchor):
    facets = lax.axis_size("facet")
    bands = lax.axis_size("freq")
    rows = visibility.shape[2]
    scale = 1.0 / (SUB * math.sqrt(facets * bands * rows))
    kept = KS // bands
    band_rows = TROWS // bands
    vmem = pl.BlockSpec(memory_space=pltpu.VMEM)
    return pl.pallas_call(
        functools.partial(kernel, facets, bands, scale),
        out_shape=jax.ShapeDtypeStruct((band_rows, TCOLS), F32),
        in_specs=[vmem, vmem, vmem, vmem, pl.BlockSpec(memory_space=pltpu.SMEM), pl.BlockSpec(memory_space=pl.ANY)],
        out_specs=vmem,
        scratch_shapes=[
            pltpu.VMEM((2, PLANES * SUB, SUB), BF16),
            pltpu.VMEM((2 * SUB, PLANES * SUB), BF16),
            pltpu.VMEM((facets, 1, LANES), F32),
            pltpu.VMEM((facets, 1, LANES), F32),
            pltpu.VMEM((2 * SUB, RADIX * 2 * TCOLS), BF16),
            pltpu.VMEM((6, SUB // bands // 2, 2 * SUB), BF16),
            pltpu.VMEM((6, SUB // bands // 2, 2 * SUB), BF16),
            pltpu.VMEM((RADIX, RADIX, 2 * kept, TCOLS), BF16),
            pltpu.VMEM((facets, 2 * kept, TCOLS), BF16),
            pltpu.VMEM((bands, 2, band_rows, facets * 2 * kept), BF16),
            pltpu.VMEM((SECTIONS, 6, band_rows // SECTIONS // 2, 2 * TCOLS), BF16),
            pltpu.VMEM((SECTIONS, 6, band_rows // SECTIONS // 2, 2 * TCOLS), BF16),
            pltpu.VMEM((SECTIONS, 7, band_rows // SECTIONS, TCOLS), BF16),
            pltpu.VMEM((SECTIONS, 7, band_rows // SECTIONS, TCOLS), BF16),
            pltpu.SemaphoreType.DMA,
            pltpu.SemaphoreType.DMA((2,)),
            pltpu.SemaphoreType.DMA((2,)),
            pltpu.SemaphoreType.DMA((2, 6)),
            pltpu.SemaphoreType.DMA((2, SECTIONS, 6)),
            pltpu.SemaphoreType.DMA((2, SECTIONS, 7)),
        ],
        compiler_params=pltpu.CompilerParams(
            collective_id=0, has_side_effects=True, vmem_limit_bytes=60 * 1024 * 1024
        ),
        cost_estimate=pl.CostEstimate(flops=8 * 10**9, bytes_accessed=4 * 10**6, transcendentals=0),
    )(
        visibility[0], row_target.reshape(1, rows), row_cell, row_plane, subgrid_anchor, kernel_table
    )


def solution(mesh):
    placed = (
        P("freq", None, "facet"),
        P("freq", "facet", None),
        P("freq", "facet"),
        P("freq", "facet"),
        P(),
        P("facet", None),
    )
    return jax.shard_map(
        shards, mesh=mesh, in_specs=placed, out_specs=P(("facet", "freq"), None), check_vma=False
    )
```

time: 65.6 us -> 60.5 us (0.922)
  the two profiles are of different devices: /device:TPU:1 before, /device:TPU:8 now
where the time goes in v2:
time: 60.5 us; the launch traced here: 60.4 us
  Pallas kernels  58.8 us (97%)
  local copies, waits for them, and re-layouts  1.57 us (3%)
    pallas_call x1, Pallas kernels, shards(): pl.pallas_call(functools.partial(kernel, facets, bands, scale), out_shape...  58.8 us
    unnamed x1, local copies, waits for them, and re-layouts  1.57 us

profile of v2, /device:TPU:8, one launch (start us, length us, event | category | flops | bytes accessed | tf_op | source)
XLA Modules:
  0.0 60.4 jit_solution(8234875832837187217)
XLA Ops:
  0.0 58.8 %shard_map.64 = f32[256,128]{1,0:T(8,128)} custom-call(bf16[2,512]{1,0:T(2,128)(2,1)} %bitcast.2, s32[1,512]{1,0:T(1,128)} %bitcast.3, s32[1,512]{1,0:T(1,128)} %cell_ref.1, s32[1,512]{1,0:T(1,128)} %plane_ref.1, s32[1,2]{1,0:T(1,128)} %anchor_ref.1, bf16[2,2048,256]{2,1,0:T(8,128)(2,1)} %table_hbm.1), custom_call_target="tpu_custom_call" | custom-call | flops 8000000000 | bytes 4000000 | tf_op jit(solution)/shard_map/pallas_call | solution.py:368
  58.9 1.6 %copy.8 = f32[256,128]{1,0:T(8,128)} copy(f32[256,128]{1,0:T(8,128)} %shard_map.64) | data formatting | bytes 262144

commit v3 on v2

--- a/solution.py
+++ b/solution.py
@@ -105,8 +105,9 @@
 ):
     me = lax.axis_index("facet")
     band = lax.axis_index("freq")
-    my_class, my_column = me // RADIX, me % RADIX
-    my_z, my_y = my_class // 4, my_class % 4
+    my_share, my_column = me // RADIX, me % RADIX
+    my_z, my_y = my_share // 4, my_share % 4
+    special = jnp.where(my_y == 0, 1, 0)
     rows = vis_ref.shape[1]
     cells = PLANES * SUB
     band_rows = TROWS // bands
@@ -162,18 +163,23 @@
             device_id={"facet": lax.rem(me + 1, facets)}, device_id_type=MESH,
         )
 
+    low = iota((1, TCOLS), 1) < TCOLS // 2
+
+    def swap(value):
+        return pltpu.roll(value, TCOLS // 2, 1)
+
     for step in range(RADIX):
         group = lax.rem(my_column + step, RADIX)
         spatial = vs + iota((SUB, TCOLS), 0)
         pixel = iota((SUB, TCOLS), 1)
         index = (((spatial & (RADIX - 1)) * group & (RADIX - 1)) << 13) + spatial * pixel
         cos_r, sin_r = turn(index)
-        cos_r, sin_r = cos_r.astype(BF16), sin_r.astype(BF16)
+        cos_s, sin_s = swap(cos_r), swap(sin_r)
         at = step * 2 * TCOLS
-        right[:SUB, at:at + TCOLS] = cos_r
-        right[:SUB, at + TCOLS:at + 2 * TCOLS] = sin_r
-        right[SUB:, at:at + TCOLS] = -sin_r
-        right[SUB:, at + TCOLS:at + 2 * TCOLS] = cos_r
+        right[:SUB, at:at + TCOLS] = jnp.where(low, cos_r, sin_s).astype(BF16)
+        right[:SUB, at + TCOLS:at + 2 * TCOLS] = jnp.where(low, cos_s, sin_r).astype(BF16)
+        right[SUB:, at:at + TCOLS] = jnp.where(low, -sin_r, cos_s).astype(BF16)
+        right[SUB:, at + TCOLS:at + 2 * TCOLS] = jnp.where(low, -sin_s, cos_r).astype(BF16)
 
     load_table.wait()
     place = iota((SUB, SUB), 0)
@@ -218,51 +224,64 @@
     width = facets * 2 * kept
     own_s = iota((facets, width), 0) == (iota((facets, width), 1) >> 4)
     first = jnp.sum(jnp.where(own_s, got[:, 5 * CAP:5 * CAP + 1], 0.0), axis=0, keepdims=True).astype(I32)
-    first = first + ((my_class - first) & (RADIX - 1))
     column = iota((1, width), 1)
-    spatial = first + (((column & (kept - 1)) + band * kept) << 3)
-    ahead = ((column >> 3) & 1) << 14
+    second = (column >> 3) & 1
+    wanted = my_y + second * (RADIX - 2 * my_y)
+    sign = 1 - 2 * second * (1 - special)
     fine = 32
     pieces = band_rows // fine
     coarse = iota((bands * pieces, width), 0)
     coarse = ((((coarse >> 3) + band) & (bands - 1)) << 3) + (coarse & (pieces - 1))
 
-    def make_left(blocks):
-        for piece in range(blocks[0] * pieces, (blocks[-1] + 1) * pieces):
-            p_r, p_i = coarse_r[piece:piece + 1], coarse_i[piece:piece + 1]
+    def tables(residue, ahead):
+        spatial = first + ((residue - first) & (RADIX - 1)) + (((column & (kept - 1)) + band * kept) << 3)
+        spatial = (spatial * sign) & (NGRID - 1)
+        return *turn(coarse * fine * spatial), *turn(iota((fine, width), 0) * spatial + ahead)
+
+    def make_left():
+        for piece in range(bands * pieces):
             block, at = piece // pieces, piece % pieces * fine
-            left[block, 0, at:at + fine] = (p_r * fine_r - p_i * fine_i).astype(BF16)
-            left[block, 1, at:at + fine] = (p_r * fine_i + p_i * fine_r).astype(BF16)
+            c_r, c_i, f_r, f_i = tables_cos
+            left[block, 0, at:at + fine] = (c_r[piece:piece + 1] * f_r - c_i[piece:piece + 1] * f_i).astype(BF16)
+            c_r, c_i, f_r, f_i = tables_sin
+            left[block, 1, at:at + fine] = (c_r[piece:piece + 1] * f_i + c_i[piece:piece + 1] * f_r).astype(BF16)
 
     ring = RingSum(grid_chunk, band_up, band_down, grid_out, grid_in, grid_sems.at[0], grid_sems.at[1])
     ring.start()
     ring.plain()
-    coarse_r, coarse_i = turn(coarse * fine * spatial)
-    fine_r, fine_i = turn(iota((fine, width), 0) * spatial + ahead)
+    tables_cos = tables(wanted, (special * second) << 14)
+    tables_sin = tables(wanted + 4 * special, (special * (second + 1)) << 14)
     ring.middle()
-    make_left(range(bands))
+    make_left()
     grid = ring.finish().astype(BF16)
 
-    share = RADIX // 2
+    some = RADIX // 2
+    conjugate = jnp.where(low, 1.0, -1.0)
     for part in range(2):
-        span = share * 2 * TCOLS
+        span = some * 2 * TCOLS
         half = dot(grid, right[:, part * span:(part + 1) * span])
-        for step in range(share):
-            at = step * 2 * TCOLS
-            pieces = [half[:, at + p * TCOLS:at + (p + 1) * TCOLS].reshape(RADIX, kept, TCOLS) for p in range(2)]
-            send2[part * share + step] = jnp.concatenate(pieces, axis=1).astype(BF16)
-
-        @pl.loop(0, share * RADIX)
+        for step in range(some):
+            for z in range(2):
+                at = (step * 2 + z) * TCOLS
+                rows_of = [half[c * kept:(c + 1) * kept, at:at + TCOLS] for c in range(RADIX)]
+                shares = [
+                    (jnp.where(low, rows_of[0], swap(rows_of[4])), jnp.where(low, swap(rows_of[0]), rows_of[4])),
+                    *((rows_of[c], rows_of[RADIX - c] * conjugate) for c in range(1, 4)),
+                ]
+                for y in range(4):
+                    send2[part * some + step, z * 4 + y] = jnp.concatenate(shares[y], axis=0).astype(BF16)
+
+        @pl.loop(0, some * RADIX)
         def _(number):
-            step, turn_by = part * share + number // RADIX, number % RADIX
-            peer_class = lax.rem(my_class + turn_by, RADIX)
-            peer = peer_class * RADIX + lax.rem(my_column + step, RADIX)
+            step, turn_by = part * some + number // RADIX, number % RADIX
+            peer_share = lax.rem(my_share + turn_by, RADIX)
+            peer = peer_share * RADIX + lax.rem(my_column + step, RADIX)
 
             @pl.when(peer != me)
             def _():
-                send(send2.at[step, peer_class], recv2.at[me], send_sems.at[1], recv_sems.at[1], {"facet": peer})
-
-    recv2[pl.ds(me, 1)] = send2[0, pl.ds(my_class, 1)]
+                send(send2.at[step, peer_share], recv2.at[me], send_sems.at[1], recv_sems.at[1], {"facet": peer})
+
+    recv2[pl.ds(me, 1)] = send2[0, pl.ds(my_share, 1)]
 
     wait2 = settle(recv2, 1)
     wait2.wait_recv()
@@ -274,25 +293,36 @@
     y_up, y_down = lax.rem(my_y + 1, 4), lax.rem(my_y + 3, 4)
     across = lax.rem(my_y + 2, 4)
 
+    spec = special.astype(F32)
+    below = jnp.where(low, 1.0, 0.0)
+    plain = 1.0 - spec * (1.0 - below)
+    kept_sine = spec * (1.0 - below)
+    turned_sine = (1.0 - spec) * (1.0 - 2.0 * below)
+
     def tile_part(section, r, h):
         at = section * section_rows + h * half_rows
-        return jnp.concatenate([dot(left[r, p, at:at + half_rows], mixed) for p in range(2)], axis=1)
+        cosines, sines = [dot(left[r, p, at:at + half_rows], mixed) for p in range(2)]
+        return cosines * plain + sines * kept_sine + swap(sines) * turned_sine
 
     def phase(z, y):
-        return turn(jnp.zeros((1, TCOLS), I32) + ((my_class * (4 * z + y) & (RADIX - 1)) << 13))
+        cos_c, sin_c = turn(jnp.zeros((1, TCOLS), I32) + ((my_y * (4 * z + y) & (RADIX - 1)) << 13))
+        other = special * (1 - 2 * (y & 1))
+        other = other.astype(F32) - sin_c
+        return jnp.where(low, cos_c, other), jnp.where(low, other, cos_c)
 
     phases = {(z, n): phase(z, y) for z in range(2) for n, y in enumerate((my_y, y_up, across, y_down))}
     phases["pair"], phases["own"] = phase(1 - my_z, my_y), phase(my_z, my_y)
 
     class Last:
         def __init__(self, section, total):
-            self.real, self.imag = total[:, :TCOLS], total[:, TCOLS:]
+            self.total, self.swapped = total, swap(total)
             self.out, self.came = last_out.at[section], last_in.at[section]
             self.send_sem, self.recv_sem = last_sems.at[0, section], last_sems.at[1, section]
             self.copies = []
 
         def turned(self, key):
-            return self.real * phases[key][0] - self.imag * phases[key][1]
+            both = self.total * phases[key][0] + self.swapped * phases[key][1]
+            return jnp.where(low, both[:half_rows], both[half_rows:])
 
         def go(self, out_slot, in_slot, value, z, y):
             self.out[out_slot] = value.astype(BF16)
@@ -322,10 +352,13 @@
             self.go(5, 4 + my_z, term_down + self.arrived(1), 1, y_down)
 
         def finish(self):
-            image = self.turned("own")
-            for slot in range(2, 7):
-                image = image + self.arrived(slot)
-            return image
+            came = [None, None, *(self.arrived(slot) for slot in range(2, 7))]
+            own = self.turned("own")
+            first = came[2] + came[4] + jnp.where(my_z == 0, own, came[6])
+            other = came[3] + came[5] + jnp.where(my_z == 0, came[6], own)
+            return jnp.concatenate(
+                [jnp.where(low, first, swap(other)), jnp.where(low, swap(first), other)], axis=0
+            )
 
     rings = [
         RingSum(
@@ -381,10 +414,10 @@
             pltpu.VMEM((RADIX, RADIX, 2 * kept, TCOLS), BF16),
             pltpu.VMEM((facets, 2 * kept, TCOLS), BF16),
             pltpu.VMEM((bands, 2, band_rows, facets * 2 * kept), BF16),
-            pltpu.VMEM((SECTIONS, 6, band_rows // SECTIONS // 2, 2 * TCOLS), BF16),
-            pltpu.VMEM((SECTIONS, 6, band_rows // SECTIONS // 2, 2 * TCOLS), BF16),
-            pltpu.VMEM((SECTIONS, 7, band_rows // SECTIONS, TCOLS), BF16),
-            pltpu.VMEM((SECTIONS, 7, band_rows // SECTIONS, TCOLS), BF16),
+            pltpu.VMEM((SECTIONS, 6, band_rows // SECTIONS // 2, TCOLS), BF16),
+            pltpu.VMEM((SECTIONS, 6, band_rows // SECTIONS // 2, TCOLS), BF16),
+            pltpu.VMEM((SECTIONS, 7, band_rows // SECTIONS // 2, TCOLS), BF16),
+            pltpu.VMEM((SECTIONS, 7, band_rows // SECTIONS // 2, TCOLS), BF16),
             pltpu.SemaphoreType.DMA,
             pltpu.SemaphoreType.DMA((2,)),
             pltpu.SemaphoreType.DMA((2,)),

time: 60.5 us -> 56.3 us (0.931)
  Pallas kernels: 58.8 us -> 54.3 us
    pallas_call x1, Pallas kernels: 58.8 us -> 54.3 us  [shards(): pl.pallas_call(functools.partial(kernel, facets, bands, scale), out_shape...]
where the time goes in v3:
time: 56.3 us; the launch traced here: 55.8 us
  Pallas kernels  54.3 us (96%)
  local copies, waits for them, and re-layouts  1.57 us (3%)
    pallas_call x1, Pallas kernels, shards(): pl.pallas_call(functools.partial(kernel, facets, bands, scale), out_shape...  54.3 us
    unnamed x1, local copies, waits for them, and re-layouts  1.57 us

profile of v3, /device:TPU:8, one launch (start us, length us, event | category | flops | bytes accessed | tf_op | source)
XLA Modules:
  0.0 55.8 jit_solution(6601511805677011875)
XLA Ops:
  0.0 54.3 %shard_map.64 = f32[256,128]{1,0:T(8,128)} custom-call(bf16[2,512]{1,0:T(2,128)(2,1)} %bitcast.2, s32[1,512]{1,0:T(1,128)} %bitcast.3, s32[1,512]{1,0:T(1,128)} %cell_ref.1, s32[1,512]{1,0:T(1,128)} %plane_ref.1, s32[1,2]{1,0:T(1,128)} %anchor_ref.1, bf16[2,2048,256]{2,1,0:T(8,128)(2,1)} %table_hbm.1), custom_call_target="tpu_custom_call" | custom-call | flops 8000000000 | bytes 4000000 | tf_op jit(solution)/shard_map/pallas_call | solution.py:401
  54.3 1.6 %copy.8 = f32[256,128]{1,0:T(8,128)} copy(f32[256,128]{1,0:T(8,128)} %shard_map.64) | data formatting | bytes 262144

commit v4 on v3

--- a/solution.py
+++ b/solution.py
@@ -18,6 +18,11 @@
 LANES = 128
 KS = SUB // RADIX
 SECTIONS = 2
+PLACES = sorted(
+    ((z, y, x, c) for z in range(2) for y in range(4) for x in range(4) for c in range(2) if z + y + x + c),
+    key=lambda p: -(2 * p[0] + 2 * min(p[1], 4 - p[1]) + 2 * min(p[2], 4 - p[2]) + p[3]),
+)
+COLUMNS = tuple((x, c) for x in (2, 1, 3, 0) for c in (1, 0))
 MESH = pl.DeviceIdType.MESH
 F32, BF16, I32 = jnp.float32, jnp.bfloat16, jnp.int32
 
@@ -99,15 +104,16 @@
 
 def kernel(
     facets, bands, scale,
-    vis_ref, target_ref, cell_ref, plane_ref, anchor_ref, table_hbm, out_ref,
-    table, ordered, send1, recv1, right, grid_out, grid_in, send2, recv2, left, part_out, part_in, last_out, last_in,
-    table_sem, send_sems, recv_sems, grid_sems, part_sems, last_sems,
+    vis_hbm, target_hbm, cell_hbm, plane_hbm, anchor_hbm, table_hbm, out_ref,
+    vis_ref, target_ref, cell_ref, plane_ref, anchor_ref, table, ordered, send1, recv1, right, grid_out, grid_in, send2, recv2, left, part_out, part_in, last_out, last_in,
+    load_sems, table_sem, send_sems, recv_sems, grid_sems, part_sems, last_sems,
 ):
     me = lax.axis_index("facet")
     band = lax.axis_index("freq")
     my_share, my_column = me // RADIX, me % RADIX
     my_z, my_y = my_share // 4, my_share % 4
     special = jnp.where(my_y == 0, 1, 0)
+    my_x, my_core = my_column // 2, my_column % 2
     rows = vis_ref.shape[1]
     cells = PLANES * SUB
     band_rows = TROWS // bands
@@ -115,19 +121,33 @@
     band_up = {"freq": lax.rem(band + 1, bands)}
     band_down = {"freq": lax.rem(band + bands - 1, bands)}
 
+    pairs = (
+        (vis_hbm, vis_ref), (target_hbm, target_ref), (cell_hbm, cell_ref), (plane_hbm, plane_ref),
+        (anchor_hbm, anchor_ref),
+    )
+    loads = [pltpu.make_async_copy(*pair, load_sems.at[number]) for number, pair in enumerate(pairs)]
+    for load in loads:
+        load.start()
     load_table = pltpu.make_async_copy(table_hbm, table, table_sem)
     load_table.start()
 
     barrier = pltpu.get_barrier_semaphore()
 
-    @pl.loop(1, facets)
-    def _(offset):
-        pl.semaphore_signal(
-            barrier, inc=1, device_id={"facet": lax.rem(me + offset, facets)}, device_id_type=MESH
-        )
+
+    def column_at(x, c):
+        return lax.rem(my_x + x, 4) * 2 + lax.rem(my_core + c, 2)
+
+    def facet_at(z, y, x, c):
+        return (lax.rem(my_z + z, 2) * 4 + lax.rem(my_y + y, 4)) * RADIX + column_at(x, c)
+
+    for place in PLACES:
+        pl.semaphore_signal(barrier, inc=1, device_id={"facet": facet_at(*place)}, device_id_type=MESH)
 
     pl.semaphore_signal(barrier, inc=1, device_id=band_up, device_id_type=MESH)
     pl.semaphore_signal(barrier, inc=1, device_id=band_down, device_id_type=MESH)
+
+    for load in loads:
+        load.wait()
 
     named = iota((facets, rows), 0) == target_ref[...]
     named_f = jnp.where(named, 1.0, 0.0)
@@ -151,9 +171,8 @@
 
     pl.semaphore_wait(barrier, facets - 1 + 2)
 
-    @pl.loop(1, facets)
-    def _(offset):
-        peer = lax.rem(me + offset, facets)
+    for place in PLACES:
+        peer = facet_at(*place)
         send(send1.at[peer], recv1.at[me], send_sems.at[0], recv_sems.at[0], {"facet": peer})
 
     def settle(target, phase):
@@ -169,7 +188,7 @@
         return pltpu.roll(value, TCOLS // 2, 1)
 
     for step in range(RADIX):
-        group = lax.rem(my_column + step, RADIX)
+        group = column_at(*COLUMNS[step])
         spatial = vs + iota((SUB, TCOLS), 0)
         pixel = iota((SUB, TCOLS), 1)
         index = (((spatial & (RADIX - 1)) * group & (RADIX - 1)) << 13) + spatial * pixel
@@ -193,17 +212,22 @@
     wait1.wait_recv()
 
     got = recv1[...].reshape(facets, LANES)
+    every = iota((facets, cells), 1).astype(F32)
     v_cell = got[:, 3 * CAP:4 * CAP] + got[:, 4 * CAP:5 * CAP] * SUB
-    every = iota((facets, cells), 1).astype(F32)
-    pick_v = jnp.concatenate(
-        [jnp.where(every == v_cell[:, q:q + 1], 1.0, 0.0).astype(BF16) for q in range(CAP)], axis=0
-    )
-    k_real = dot(pick_v, table[0])
-    k_imag = dot(pick_v, table[1])
-    v_real = jnp.concatenate([got[:, q:q + 1] for q in range(CAP)], axis=0)
-    v_imag = jnp.concatenate([got[:, CAP + q:CAP + q + 1] for q in range(CAP)], axis=0)
-    b_real = (v_real * k_real - v_imag * k_imag).astype(BF16)
-    b_imag = (v_real * k_imag + v_imag * k_real).astype(BF16)
+    b_parts = []
+    for q0 in range(0, CAP, 4):
+        pick_v = jnp.concatenate(
+            [jnp.where(every == v_cell[:, q:q + 1], 1.0, 0.0).astype(BF16) for q in range(q0, q0 + 4)], axis=0
+        )
+        k_real = dot(pick_v, table[0])
+        k_imag = dot(pick_v, table[1])
+        v_real = jnp.concatenate([got[:, q:q + 1] for q in range(q0, q0 + 4)], axis=0)
+        v_imag = jnp.concatenate([got[:, CAP + q:CAP + q + 1] for q in range(q0, q0 + 4)], axis=0)
+        b_parts.append(
+            ((v_real * k_real - v_imag * k_imag).astype(BF16), (v_real * k_imag + v_imag * k_real).astype(BF16))
+        )
+    b_real = jnp.concatenate([part[0] for part in b_parts], axis=0)
+    b_imag = jnp.concatenate([part[1] for part in b_parts], axis=0)
     flat = got.T
     u_row = jnp.concatenate([flat[2 * CAP + q:2 * CAP + q + 1] for q in range(CAP)], axis=1)
     plane_row = jnp.concatenate([flat[4 * CAP + q:4 * CAP + q + 1] for q in range(CAP)], axis=1)
@@ -242,9 +266,9 @@
         for piece in range(bands * pieces):
             block, at = piece // pieces, piece % pieces * fine
             c_r, c_i, f_r, f_i = tables_cos
-            left[block, 0, at:at + fine] = (c_r[piece:piece + 1] * f_r - c_i[piece:piece + 1] * f_i).astype(BF16)
+            left[block, at:at + fine] = (c_r[piece:piece + 1] * f_r - c_i[piece:piece + 1] * f_i).astype(BF16)
             c_r, c_i, f_r, f_i = tables_sin
-            left[block, 1, at:at + fine] = (c_r[piece:piece + 1] * f_i + c_i[piece:piece + 1] * f_r).astype(BF16)
+            left[block, band_rows + at:band_rows + at + fine] = (c_r[piece:piece + 1] * f_i + c_i[piece:piece + 1] * f_r).astype(BF16)
 
     ring = RingSum(grid_chunk, band_up, band_down, grid_out, grid_in, grid_sems.at[0], grid_sems.at[1])
     ring.start()
@@ -271,17 +295,15 @@
                 for y in range(4):
                     send2[part * some + step, z * 4 + y] = jnp.concatenate(shares[y], axis=0).astype(BF16)
 
-        @pl.loop(0, some * RADIX)
-        def _(number):
-            step, turn_by = part * some + number // RADIX, number % RADIX
-            peer_share = lax.rem(my_share + turn_by, RADIX)
-            peer = peer_share * RADIX + lax.rem(my_column + step, RADIX)
-
-            @pl.when(peer != me)
-            def _():
-                send(send2.at[step, peer_share], recv2.at[me], send_sems.at[1], recv_sems.at[1], {"facet": peer})
-
-    recv2[pl.ds(me, 1)] = send2[0, pl.ds(my_share, 1)]
+        for place in PLACES:
+            step = COLUMNS.index(place[2:])
+            if step // some == part:
+                peer = facet_at(*place)
+                send(
+                    send2.at[step, peer // RADIX], recv2.at[me], send_sems.at[1], recv_sems.at[1], {"facet": peer}
+                )
+
+    recv2[pl.ds(me, 1)] = send2[COLUMNS.index((0, 0)), pl.ds(my_share, 1)]
 
     wait2 = settle(recv2, 1)
     wait2.wait_recv()
@@ -299,10 +321,15 @@
     kept_sine = spec * (1.0 - below)
     turned_sine = (1.0 - spec) * (1.0 - 2.0 * below)
 
+    tiles = {}
+
     def tile_part(section, r, h):
+        if r not in tiles:
+            both = dot(left[r], mixed)
+            cosines, sines = both[:band_rows], both[band_rows:]
+            tiles[r] = cosines * plain + sines * kept_sine + swap(sines) * turned_sine
         at = section * section_rows + h * half_rows
-        cosines, sines = [dot(left[r, p, at:at + half_rows], mixed) for p in range(2)]
-        return cosines * plain + sines * kept_sine + swap(sines) * turned_sine
+        return tiles[r][at:at + half_rows]
 
     def phase(z, y):
         cos_c, sin_c = turn(jnp.zeros((1, TCOLS), I32) + ((my_y * (4 * z + y) & (RADIX - 1)) << 13))
@@ -400,10 +427,15 @@
     vmem = pl.BlockSpec(memory_space=pltpu.VMEM)
     return pl.pallas_call(
         functools.partial(kernel, facets, bands, scale),
-        out_shape=jax.ShapeDtypeStruct((band_rows, TCOLS), F32),
-        in_specs=[vmem, vmem, vmem, vmem, pl.BlockSpec(memory_space=pltpu.SMEM), pl.BlockSpec(memory_space=pl.ANY)],
+        out_shape=pltpu.VMEM((band_rows, TCOLS), F32),
+        in_specs=[pl.BlockSpec(memory_space=pl.ANY)] * 6,
         out_specs=vmem,
         scratch_shapes=[
+            pltpu.VMEM((2, rows), BF16),
+            pltpu.VMEM((1, rows), I32),
+            pltpu.VMEM((1, rows), I32),
+            pltpu.VMEM((1, rows), I32),
+            pltpu.SMEM((1, 2), I32),
             pltpu.VMEM((2, PLANES * SUB, SUB), BF16),
             pltpu.VMEM((2 * SUB, PLANES * SUB), BF16),
             pltpu.VMEM((facets, 1, LANES), F32),
@@ -413,11 +445,12 @@
             pltpu.VMEM((6, SUB // bands // 2, 2 * SUB), BF16),
             pltpu.VMEM((RADIX, RADIX, 2 * kept, TCOLS), BF16),
             pltpu.VMEM((facets, 2 * kept, TCOLS), BF16),
-            pltpu.VMEM((bands, 2, band_rows, facets * 2 * kept), BF16),
+            pltpu.VMEM((bands, 2 * band_rows, facets * 2 * kept), BF16),
             pltpu.VMEM((SECTIONS, 6, band_rows // SECTIONS // 2, TCOLS), BF16),
             pltpu.VMEM((SECTIONS, 6, band_rows // SECTIONS // 2, TCOLS), BF16),
             pltpu.VMEM((SECTIONS, 7, band_rows // SECTIONS // 2, TCOLS), BF16),
             pltpu.VMEM((SECTIONS, 7, band_rows // SECTIONS // 2, TCOLS), BF16),
+            pltpu.SemaphoreType.DMA((5,)),
             pltpu.SemaphoreType.DMA,
             pltpu.SemaphoreType.DMA((2,)),
             pltpu.SemaphoreType.DMA((2,)),

time: 56.3 us -> 52.3 us (0.929)
  Pallas kernels: 54.3 us -> 51.6 us
  local copies, waits for them, and re-layouts: 1.57 us -> 0.66 us
    pallas_call x1, Pallas kernels: 54.3 us -> 51.6 us  [shards(): pl.pallas_call(functools.partial(kernel, facets, bands, scale), out_shape...]
    unnamed x1, local copies, waits for them, and re-layouts: 1.57 us -> 0.66 us
where the time goes in v4:
time: 52.3 us
  Pallas kernels  51.6 us (99%)
  local copies, waits for them, and re-layouts  0.66 us (1%)
    pallas_call x1, Pallas kernels, shards(): pl.pallas_call(functools.partial(kernel, facets, bands, scale), out_shape...  51.6 us

profile of v4, /device:TPU:8, one launch (start us, length us, event | category | flops | bytes accessed | tf_op | source)
XLA Modules:
  0.0 52.3 jit_solution(15320728076543977036)
XLA Ops:
  0.0 51.6 %shard_map.64 = f32[256,128]{1,0:T(8,128)S(1)} custom-call(bf16[2,512]{1,0:T(2,128)(2,1)} %bitcast.2, s32[1,512]{1,0:T(1,128)} %bitcast.3, s32[1,512]{1,0:T(1,128)} %cell_hbm.1, s32[1,512]{1,0:T(1,128)} %plane_hbm.1, s32[1,2]{1,0:T(1,128)} %anchor_hbm.1, bf16[2,2048,256]{2,1,0:T(8,128)(2,1)} %table_hbm.1), custom_call_target="tpu_custom_call" | custom-call | flops 8000000000 | bytes 4000000 | tf_op jit(solution)/shard_map/pallas_call | solution.py:428
  51.6 0.7 %copy.8 = f32[256,128]{1,0:T(8,128)} copy(f32[256,128]{1,0:T(8,128)S(1)} %shard_map.64) | data formatting | bytes 262144

commit v5 on v4

--- a/solution.py
+++ b/solution.py
@@ -202,11 +202,14 @@
 
     load_table.wait()
     place = iota((SUB, SUB), 0)
-    row_k = (((place >> 6) + band) & (bands - 1)) * kept + (place & (kept - 1))
+    row_k = ((2 - (place >> 6) + band) & (bands - 1)) * kept + (place & (kept - 1))
     wanted = (row_k << 3) + ((((place >> 3) & (RADIX - 1)) - us) & (RADIX - 1))
     order = jnp.where(iota((SUB, SUB), 1) == wanted, 1.0, 0.0).astype(BF16)
+    half_sub = SUB // 2
     for part in range(2):
-        ordered[part * SUB:(part + 1) * SUB] = nt_dot(order, table[part]).astype(BF16)
+        moved = nt_dot(order, table[part]).astype(BF16)
+        for pair in range(2):
+            ordered[pair, part * half_sub:(part + 1) * half_sub] = moved[pair * half_sub:(pair + 1) * half_sub]
 
     wait1 = settle(recv1, 0)
     wait1.wait_recv()
@@ -235,15 +238,18 @@
     pick_u = jnp.concatenate(
         [pick_u * jnp.where(plane_row == p, 1.0, 0.0).astype(BF16) for p in range(PLANES)], axis=0
     )
-    a_both = dot(ordered[...], pick_u).astype(BF16)
     b_wide = jnp.concatenate([b_real, b_imag], axis=1)
     b_turned = jnp.concatenate([-b_imag, b_real], axis=1)
     quarter = SUB // bands
-    gridded = dot(a_both[:SUB], b_wide) + dot(a_both[SUB:], b_turned)
+    made = {}
 
     def grid_chunk(r, h):
-        start = r * quarter + h * (quarter // 2)
-        return gridded[start:start + quarter // 2]
+        pair, which = divmod((2 - r) % bands, 2)
+        if pair not in made:
+            a_pair = dot(ordered[pair], pick_u).astype(BF16)
+            made[pair] = dot(a_pair[:half_sub], b_wide) + dot(a_pair[half_sub:], b_turned)
+        start = which * quarter + h * (quarter // 2)
+        return made[pair][start:start + quarter // 2]
 
     width = facets * 2 * kept
     own_s = iota((facets, width), 0) == (iota((facets, width), 1) >> 4)
@@ -279,9 +285,9 @@
     make_left()
     grid = ring.finish().astype(BF16)
 
-    some = RADIX // 2
+    some = RADIX // 4
     conjugate = jnp.where(low, 1.0, -1.0)
-    for part in range(2):
+    for part in range(4):
         span = some * 2 * TCOLS
         half = dot(grid, right[:, part * span:(part + 1) * span])
         for step in range(some):
@@ -437,7 +443,7 @@
             pltpu.VMEM((1, rows), I32),
             pltpu.SMEM((1, 2), I32),
             pltpu.VMEM((2, PLANES * SUB, SUB), BF16),
-            pltpu.VMEM((2 * SUB, PLANES * SUB), BF16),
+            pltpu.VMEM((2, SUB, PLANES * SUB), BF16),
             pltpu.VMEM((facets, 1, LANES), F32),
             pltpu.VMEM((facets, 1, LANES), F32),
             pltpu.VMEM((2 * SUB, RADIX * 2 * TCOLS), BF16),

time: 52.3 us -> 50.3 us (0.962)
  Pallas kernels: 51.6 us -> 49.5 us
    pallas_call x1, Pallas kernels: 51.6 us -> 49.5 us  [shards(): pl.pallas_call(functools.partial(kernel, facets, bands, scale), out_shape...]
where the time goes in v5:
time: 50.3 us; the launch traced here: 50.2 us
  Pallas kernels  49.5 us (98%)
  local copies, waits for them, and re-layouts  0.66 us (1%)
    pallas_call x1, Pallas kernels, shards(): pl.pallas_call(functools.partial(kernel, facets, bands, scale), out_shape...  49.5 us

profile of v5, /device:TPU:8, one launch (start us, length us, event | category | flops | bytes accessed | tf_op | source)
XLA Modules:
  0.0 50.2 jit_solution(8566303176455949473)
XLA Ops:
  0.0 49.5 %shard_map.64 = f32[256,128]{1,0:T(8,128)S(1)} custom-call(bf16[2,512]{1,0:T(2,128)(2,1)} %bitcast.2, s32[1,512]{1,0:T(1,128)} %bitcast.3, s32[1,512]{1,0:T(1,128)} %cell_hbm.1, s32[1,512]{1,0:T(1,128)} %plane_hbm.1, s32[1,2]{1,0:T(1,128)} %anchor_hbm.1, bf16[2,2048,256]{2,1,0:T(8,128)(2,1)} %table_hbm.1), custom_call_target="tpu_custom_call" | custom-call | flops 8000000000 | bytes 4000000 | tf_op jit(solution)/shard_map/pallas_call | solution.py:434
  49.5 0.7 %copy.8 = f32[256,128]{1,0:T(8,128)} copy(f32[256,128]{1,0:T(8,128)S(1)} %shard_map.64) | data formatting | bytes 262144

commit v6 on v5

--- a/solution.py
+++ b/solution.py
@@ -18,6 +18,7 @@
 LANES = 128
 KS = SUB // RADIX
 SECTIONS = 2
+EARLY = 24
 PLACES = sorted(
     ((z, y, x, c) for z in range(2) for y in range(4) for x in range(4) for c in range(2) if z + y + x + c),
     key=lambda p: -(2 * p[0] + 2 * min(p[1], 4 - p[1]) + 2 * min(p[2], 4 - p[2]) + p[3]),
@@ -126,26 +127,27 @@
         (anchor_hbm, anchor_ref),
     )
     loads = [pltpu.make_async_copy(*pair, load_sems.at[number]) for number, pair in enumerate(pairs)]
-    for load in loads:
-        load.start()
+
+    barrier = pltpu.get_barrier_semaphore()
+
+
+    def column_at(x, c):
+        return lax.rem(my_x + x, 4) * 2 + lax.rem(my_core + c, 2)
+
+    def facet_at(z, y, x, c):
+        return (lax.rem(my_z + z, 2) * 4 + lax.rem(my_y + y, 4)) * RADIX + column_at(x, c)
+
+    for number, place in enumerate(PLACES):
+        if number == EARLY:
+            for load in loads:
+                load.start()
+        pl.semaphore_signal(barrier, inc=1, device_id={"facet": facet_at(*place)}, device_id_type=MESH)
+
+    pl.semaphore_signal(barrier, inc=1, device_id=band_up, device_id_type=MESH)
+    pl.semaphore_signal(barrier, inc=1, device_id=band_down, device_id_type=MESH)
+
     load_table = pltpu.make_async_copy(table_hbm, table, table_sem)
     load_table.start()
-
-    barrier = pltpu.get_barrier_semaphore()
-
-
-    def column_at(x, c):
-        return lax.rem(my_x + x, 4) * 2 + lax.rem(my_core + c, 2)
-
-    def facet_at(z, y, x, c):
-        return (lax.rem(my_z + z, 2) * 4 + lax.rem(my_y + y, 4)) * RADIX + column_at(x, c)
-
-    for place in PLACES:
-        pl.semaphore_signal(barrier, inc=1, device_id={"facet": facet_at(*place)}, device_id_type=MESH)
-
-    pl.semaphore_signal(barrier, inc=1, device_id=band_up, device_id_type=MESH)
-    pl.semaphore_signal(barrier, inc=1, device_id=band_down, device_id_type=MESH)
-
     for load in loads:
         load.wait()
 

time: 50.3 us -> 50.4 us (level)
  no operation moved by 1% of the time
where the time goes in v6:
time: 50.4 us; the launch traced here: 50.3 us
  Pallas kernels  49.7 us (99%)
  local copies, waits for them, and re-layouts  0.66 us (1%)
    pallas_call x1, Pallas kernels, shards(): pl.pallas_call(functools.partial(kernel, facets, bands, scale), out_shape...  49.7 us

profile of v6, /device:TPU:8, one launch (start us, length us, event | category | flops | bytes accessed | tf_op | source)
XLA Modules:
  0.0 50.3 jit_solution(9232917846917187309)
XLA Ops:
  0.0 49.7 %shard_map.64 = f32[256,128]{1,0:T(8,128)S(1)} custom-call(bf16[2,512]{1,0:T(2,128)(2,1)} %bitcast.2, s32[1,512]{1,0:T(1,128)} %bitcast.3, s32[1,512]{1,0:T(1,128)} %cell_hbm.1, s32[1,512]{1,0:T(1,128)} %plane_hbm.1, s32[1,2]{1,0:T(1,128)} %anchor_hbm.1, bf16[2,2048,256]{2,1,0:T(8,128)(2,1)} %table_hbm.1), custom_call_target="tpu_custom_call" | custom-call | flops 8000000000 | bytes 4000000 | tf_op jit(solution)/shard_map/pallas_call | solution.py:436
  49.7 0.7 %copy.8 = f32[256,128]{1,0:T(8,128)} copy(f32[256,128]{1,0:T(8,128)S(1)} %shard_map.64) | data formatting | bytes 262144
